TPU v7x, 256 devices: a whole 4x4x8 slice. The times are simulated.
256 devices in a mesh: tm: 64 (over y, x_hi, z), mode: 4 (over x_lo, core).
Axes of the slice: x: 4 (x_hi: 2, x_lo: 2; x = x_hi * 2 + x_lo), y: 4, z: 8, core: 2. Of those that a mesh axis runs over, the one named last changes fastest.
Arguments:
- fields_left: bfloat16 [2, 2, 64, 1024, 1024], P(None, None, 'tm', 'mode'), may hold values from -0.125 to 0.125
- fields_right: bfloat16 [2, 2, 64, 1024, 1024], P(None, None, 'tm', 'mode'), may hold values from -6 to 6
- delta: int32 [2], replicated, may hold values from 1 to 7, as said below
- pair: int32 [2], replicated, may hold values from 0 to 1, each once
Outputs:
- rectangle: float32 [64, 2, 2, 2, 6], P('tm')
- box: float32 [64, 2, 2, 2, 6], P('tm')
Inputs may be any that keep to these rules, and one draw needn't show every extreme that they name: `delta`: the offsets are distinct, and exactly one of them is 7. Each momentum pair is used by exactly one product.
All inputs are finite; a program needn't handle non-finite values.
Results may differ from a plain program's by a relative error of at most 0.004.
Values may be sent and summed in bfloat16 or wider, within the bound.
A program may use at most 128 MiB of HBM per device.

v0:
```python
import jax
import jax.numpy as jnp
from jax import lax
from jax.sharding import PartitionSpec as P

HALF = 3
DMAX = 7


def passed_along(value, axis, steps):
    count = lax.axis_size(axis)
    pairs = [(source, (source + steps) % count) for source in range(count)]
    return lax.ppermute(value, axis, pairs)


def complex_rect(source, sink):
    grams = jnp.einsum("kcrn,ldrn->kcld", source, sink, preferred_element_type=jnp.float32)
    real_part = grams[:, 0, :, 0] + grams[:, 1, :, 1]
    imag_part = grams[:, 1, :, 0] - grams[:, 0, :, 1]
    return jnp.stack([real_part, imag_part])


def box_terms(here, there):
    real_part = here[:, None, 0] * there[None, :, 0] + here[:, None, 1] * there[None, :, 1]
    imag_part = here[:, None, 1] * there[None, :, 0] - here[:, None, 0] * there[None, :, 1]
    return jnp.stack([real_part, imag_part])


def partial_trace(block, offset, local_rows):
    square = lax.dynamic_slice_in_dim(block, offset, local_rows, 3)
    return jnp.sum(jnp.diagonal(square, axis1=2, axis2=3).astype(jnp.float32), axis=-1)


def on_device(fields_left, fields_right, delta, pair):
    local_rows = fields_left.shape[3]
    width = fields_left.shape[4]
    left_sel = jnp.take(fields_left[:, :, 0], pair, axis=0)
    moving = jnp.take(fields_right[:, :, 0], pair, axis=0)
    for bit_index in range(DMAX.bit_length()):
        moved = passed_along(moving, "tm", -(1 << bit_index))
        use_bit = jnp.right_shift(delta, bit_index) % 2 == 1
        moving = jnp.where(use_bit[:, None, None, None], moved, moving)
    piece = lax.all_gather(moving, "mode", axis=2, tiled=True)
    real_rows = jnp.stack([piece[:, 0], -piece[:, 1]], axis=1)
    imag_rows = jnp.stack([piece[:, 1], piece[:, 0]], axis=1)
    stacked = jnp.stack([real_rows, imag_rows], axis=2)
    summed_product = jnp.einsum(
        "kcrn,kcdnm->kdrm", left_sel, stacked, preferred_element_type=jnp.float32
    )
    product = summed_product.astype(jnp.bfloat16)
    offset = lax.axis_index("mode") * local_rows
    sink = product
    rect_list = []
    trace_list = [partial_trace(product, offset, local_rows)]
    for sep_index in range(2 * HALF):
        sink = passed_along(sink, "tm", -1)
        rect_list.append(complex_rect(product, sink))
        trace_list.append(partial_trace(sink, offset, local_rows))
    partial_rect = jnp.stack(rect_list, axis=-1)
    partial_traces = jnp.stack(trace_list)
    summed_rect, summed_traces = lax.psum((partial_rect, partial_traces), "mode")
    rectangle = summed_rect / width
    box = (
        jnp.stack(
            [
                box_terms(summed_traces[0], summed_traces[sep_index])
                for sep_index in range(1, 2 * HALF + 1)
            ],
            axis=-1,
        )
        / width
    )
    return (rectangle[None], box[None])


def solution(mesh):
    in_specs = (P(None, None, "tm", "mode", None), P(None, None, "tm", "mode", None), P(), P())
    out_specs = (P("tm", None, None, None, None), P("tm", None, None, None, None))
    return jax.shard_map(
        on_device, mesh=mesh, in_specs=in_specs, out_specs=out_specs, check_vma=False
    )
```

profile of v0, /device:TPU:1, one launch (start us, length us, event | category | flops | bytes accessed | tf_op | source)
XLA Modules:
  0.0 997.5 jit_solution(7585199449513353351)
XLA Ops:
  7.2 0.8 compare_and_fusion
  8.0 0.7 compare_select_fusion
  8.8 2.0 gather_fusion.7
  10.8 2.8 copy.84
  13.7 0.3 broadcast_select_fusion
  13.9 11.4 %collective-permute-start = (bf16[2,2,256,1024]{2,3,1,0:T(8,128)(2,1)S(1)}, bf16[2,2,256,1024]{2,3,1,0:T(8,128)(2,1)S(1)}, u32[]{:S(2)}, u32[]{:S(2)}) collective-permute-start(bf16[2,2,256,1024]{2,3,1,0:T(8,128)(2,1)S(1)} %broadcast_select_fusion), channel_id=1, source_target_pairs={{0,252},{4,0},{8,4},{12,8},{16,12},{20,16},{24,20},{28,24},{32,28}... | collective-permute-start | bytes 6291464 | tf_op jit(solution)/shard_map/ppermute | solution.py:13
  25.4 44.3 %collective-permute-done = bf16[2,2,256,1024]{2,3,1,0:T(8,128)(2,1)S(1)} collective-permute-done((bf16[2,2,256,1024]{2,3,1,0:T(8,128)(2,1)S(1)}, bf16[2,2,256,1024]{2,3,1,0:T(8,128)(2,1)S(1)}, u32[]{:S(2)}, u32[]{:S(2)}) %collective-permute-start) | collective-permute-done | bytes 2097184 | tf_op jit(solution)/shard_map/ppermute | solution.py:13
  69.6 0.3 broadcast_select_fusion.1
  69.9 2.7 collective-permute-start.1
  72.7 88.2 %collective-permute-done.1 = bf16[2,2,256,1024]{2,3,1,0:T(8,128)(2,1)S(1)} collective-permute-done((bf16[2,2,256,1024]{2,3,1,0:T(8,128)(2,1)S(1)}, bf16[2,2,256,1024]{2,3,1,0:T(8,128)(2,1)S(1)}, u32[]{:S(2)}, u32[]{:S(2)}) %collective-permute-start.1) | collective-permute-done | bytes 2097184 | tf_op jit(solution)/shard_map/ppermute | solution.py:13
  160.9 0.3 broadcast_select_fusion.2
  161.3 91.8 %collective-permute-done.2 = bf16[2,2,256,1024]{2,3,1,0:T(8,128)(2,1)S(1)} collective-permute-done((bf16[2,2,256,1024]{2,3,1,0:T(8,128)(2,1)S(1)}, bf16[2,2,256,1024]{2,3,1,0:T(8,128)(2,1)S(1)}, u32[]{:S(2)}, u32[]{:S(2)}) %collective-permute-start.2) | collective-permute-done | bytes 2097184 | tf_op jit(solution)/shard_map/ppermute | solution.py:13
  253.0 1.7 broadcast_select_fusion.3
  254.7 1.6 copy-done.2
  256.3 2.0 gather_fusion.8
  258.3 91.7 %all-gather.2.cloned.1.call-done = bf16[2,2,1024,1024]{2,3,1,0:T(8,128)(2,1)} async-done(((bf16[2,2,256,1024]{2,3,1,0:T(8,128)(2,1)}), bf16[2,2,1024,1024]{2,3,1,0:T(8,128)(2,1)}) %all-gather.2.cloned.1.call-update) | async-done | bytes 8388624 | tf_op jit(solution)/shard_map/all_gather | solution.py:43
  350.0 3.9 slice_negate_fusion
  353.9 1.5 maximum_bitcast_fusion
  355.5 6.5 bitcast_convert_fusion
  362.0 7.4 collective-permute-start.3
  369.4 44.9 %collective-permute-done.3 = bf16[2,2,256,1024]{2,3,1,0:T(8,128)(2,1)S(1)} collective-permute-done((bf16[2,2,256,1024]{2,3,1,0:T(8,128)(2,1)S(1)}, bf16[2,2,256,1024]{2,3,1,0:T(8,128)(2,1)S(1)}, u32[]{:S(2)}, u32[]{:S(2)}) %collective-permute-start.3) | collective-permute-done | bytes 2097184 | tf_op jit(solution)/shard_map/ppermute | solution.py:13
  414.3 7.6 collective-permute-start.4
  421.9 44.8 %collective-permute-done.4 = bf16[2,2,256,1024]{2,3,1,0:T(8,128)(2,1)S(1)} collective-permute-done((bf16[2,2,256,1024]{2,3,1,0:T(8,128)(2,1)S(1)}, bf16[2,2,256,1024]{2,3,1,0:T(8,128)(2,1)S(1)}, u32[]{:S(2)}, u32[]{:S(2)}) %collective-permute-start.4) | collective-permute-done | bytes 2097184 | tf_op jit(solution)/shard_map/ppermute | solution.py:13
  466.7 1.3 copy-done.4
  468.1 7.9 collective-permute-start.5
  476.0 43.9 %collective-permute-done.5 = bf16[2,2,256,1024]{2,3,1,0:T(8,128)(2,1)} collective-permute-done((bf16[2,2,256,1024]{2,3,1,0:T(8,128)(2,1)S(1)}, bf16[2,2,256,1024]{2,3,1,0:T(8,128)(2,1)}, u32[]{:S(2)}, u32[]{:S(2)}) %collective-permute-start.5) | collective-permute-done | bytes 2097184 | tf_op jit(solution)/shard_map/ppermute | solution.py:13
  519.9 8.2 collective-permute-start.6
  528.1 3.5 copy.126
  531.6 40.8 %copy.104 = bf16[2,2,256,256]{1,0,3,2:T(2,128)(2,1)} copy(bf16[2,2,256,256]{2,3,1,0:T(8,128)(2,1)S(1)} %dynamic-slice_bitcast_fusion) | data formatting | bytes 1048576 | tf_op jit(solution)/shard_map/dynamic_slice | solution.py:30
  572.4 2.5 gather_fusion
  574.9 0.3 convert_reduce_fusion.6
  575.2 22.1 %fusion.20 = f32[2,2,2,2]{3,1,2,0:T(2,128)S(1)} fusion(bf16[2,2,256,1024,1]{2,1,3,4,0:T(2,128)(2,1)S(1)} %copy-done.3, bf16[2,2,256,1024]{2,3,1,0:T(8,128)(2,1)} %copy-done.5), kind=kOutput, calls=%fused_computation.40 | convolution fusion | flops 8388608 | bytes 4194368 | tf_op jit(solution)/shard_map/kcrn,ldrn->kcld/dot_general | solution.py:17
  597.7 1.1 constant_dynamic-slice_fusion.5
  598.7 40.8 %copy.105 = bf16[2,2,256,256]{1,0,3,2:T(2,128)(2,1)} copy(bf16[2,2,256,256]{2,3,1,0:T(8,128)(2,1)S(1)} %constant_dynamic-slice_fusion.5) | data formatting | bytes 1048576 | tf_op jit(solution)/shard_map/dynamic_slice | solution.py:30
  639.5 2.5 gather_fusion.1
  642.0 0.3 convert_reduce_fusion.5
  642.4 22.3 %fusion.19 = f32[2,2,2,2]{3,1,2,0:T(2,128)S(1)} fusion(bf16[2,2,256,1024,1]{2,1,3,4,0:T(2,128)(2,1)} %copy.126, bf16[2,2,256,1024]{2,3,1,0:T(8,128)(2,1)} %copy-done.4), kind=kOutput, calls=%fused_computation.39 | convolution fusion | flops 8388608 | bytes 4194368 | tf_op jit(solution)/shard_map/kcrn,ldrn->kcld/dot_general | solution.py:17
  665.0 1.1 constant_dynamic-slice_fusion.4
  666.1 40.8 %copy.106 = bf16[2,2,256,256]{1,0,3,2:T(2,128)(2,1)} copy(bf16[2,2,256,256]{2,3,1,0:T(8,128)(2,1)S(1)} %constant_dynamic-slice_fusion.4) | data formatting | bytes 1048576 | tf_op jit(solution)/shard_map/dynamic_slice | solution.py:30
  706.9 2.5 gather_fusion.2
  709.4 0.3 convert_reduce_fusion.4
  709.7 22.6 %fusion.18 = f32[2,2,2,2]{3,1,2,0:T(2,128)S(1)} fusion(bf16[2,2,256,1024,1]{2,1,3,4,0:T(2,128)(2,1)} %copy.126, bf16[2,2,256,1024]{2,3,1,0:T(8,128)(2,1)} %collective-permute-done.5), kind=kOutput, calls=%fused_computation.38 | convolution fusion | flops 8388608 | bytes 4194368 | tf_op jit(solution)/shard_map/kcrn,ldrn->kcld/dot_general | solution.py:17
  732.6 1.1 constant_dynamic-slice_fusion.3
  733.7 40.8 %copy.107 = bf16[2,2,256,256]{1,0,3,2:T(2,128)(2,1)} copy(bf16[2,2,256,256]{2,3,1,0:T(8,128)(2,1)S(1)} %constant_dynamic-slice_fusion.3) | data formatting | bytes 1048576 | tf_op jit(solution)/shard_map/dynamic_slice | solution.py:30
  774.5 2.5 gather_fusion.3
  776.9 0.3 convert_reduce_fusion.3
  777.3 22.3 %fusion.17 = f32[2,2,2,2]{3,1,2,0:T(2,128)S(1)} fusion(bf16[2,2,256,1024,1]{2,1,3,4,0:T(2,128)(2,1)} %copy.126, bf16[2,2,256,1024]{2,3,1,0:T(8,128)(2,1)} %collective-permute-done.6), kind=kOutput, calls=%fused_computation.37 | convolution fusion | flops 8388608 | bytes 4194368 | tf_op jit(solution)/shard_map/kcrn,ldrn->kcld/dot_general | solution.py:17
  800.0 1.1 constant_dynamic-slice_fusion.2
  801.1 40.8 %copy.108 = bf16[2,2,256,256]{1,0,3,2:T(2,128)(2,1)} copy(bf16[2,2,256,256]{2,3,1,0:T(8,128)(2,1)S(1)} %constant_dynamic-slice_fusion.2) | data formatting | bytes 1048576 | tf_op jit(solution)/shard_map/dynamic_slice | solution.py:30
  841.8 2.5 gather_fusion.4
  844.3 0.3 convert_reduce_fusion.2
  844.7 22.4 %fusion.16 = f32[2,2,2,2]{3,1,2,0:T(2,128)S(1)} fusion(bf16[2,2,256,1024,1]{2,1,3,4,0:T(2,128)(2,1)} %copy.126, bf16[2,2,256,1024]{2,3,1,0:T(8,128)(2,1)} %collective-permute-done.7), kind=kOutput, calls=%fused_computation.36 | convolution fusion | flops 8388608 | bytes 4194368 | tf_op jit(solution)/shard_map/kcrn,ldrn->kcld/dot_general | solution.py:17
  867.3 1.1 constant_dynamic-slice_fusion.1
  868.4 40.8 %copy.109 = bf16[2,2,256,256]{1,0,3,2:T(2,128)(2,1)} copy(bf16[2,2,256,256]{2,3,1,0:T(8,128)(2,1)S(1)} %constant_dynamic-slice_fusion.1) | data formatting | bytes 1048576 | tf_op jit(solution)/shard_map/dynamic_slice | solution.py:30
  909.2 2.5 gather_fusion.5
  911.7 0.3 convert_reduce_fusion.1
  912.1 22.4 %fusion.15 = f32[2,2,2,2]{3,1,2,0:T(2,128)S(1)} fusion(bf16[2,2,256,1024,1]{2,1,3,4,0:T(2,128)(2,1)} %copy.126, bf16[2,2,256,1024]{2,3,1,0:T(8,128)(2,1)} %collective-permute-done.8), kind=kOutput, calls=%fused_computation.35 | convolution fusion | flops 8388608 | bytes 4194368 | tf_op jit(solution)/shard_map/kcrn,ldrn->kcld/dot_general | solution.py:17
  934.8 1.1 constant_dynamic-slice_fusion
  935.9 40.8 %copy.110 = bf16[2,2,256,256]{1,0,3,2:T(2,128)(2,1)} copy(bf16[2,2,256,256]{2,3,1,0:T(8,128)(2,1)S(1)} %constant_dynamic-slice_fusion) | data formatting | bytes 1048576 | tf_op jit(solution)/shard_map/dynamic_slice | solution.py:30
  976.6 2.5 gather_fusion.6
  979.1 0.3 convert_reduce_fusion
  979.7 7.3 all-reduce
  987.0 0.6 multiply_bitcast_fusion
  989.6 0.6 broadcast_multiply_fusion
  (70 shorter events, 5.0 us)
Async XLA Ops:
  7.2 1.6 copy-start
  7.2 342.8 %all-gather.2.cloned.1.call-start = ((), (), s32[]{:S(2)}) async-start(), calls=%async_computation | async-start | bytes 10485760 | tf_op jit(solution)/shard_map/all_gather | solution.py:43
  13.7 11.7 %copy-start.6 = (s32[2]{0:T(128)S(1)}, s32[2]{0:T(128)}, u32[]{:S(2)}) copy-start(s32[2]{0:T(128)} %param.8) | copy-start | bytes 28
  13.9 55.7 %collective-permute-start = (bf16[2,2,256,1024]{2,3,1,0:T(8,128)(2,1)S(1)}, bf16[2,2,256,1024]{2,3,1,0:T(8,128)(2,1)S(1)}, u32[]{:S(2)}, u32[]{:S(2)}) collective-permute-start(bf16[2,2,256,1024]{2,3,1,0:T(8,128)(2,1)S(1)} %broadcast_select_fusion), channel_id=1, source_target_pairs={{0,252},{4,0},{8,4},{12,8},{16,12},{20,16},{24,20},{28,24},{32,28}... | collective-permute-start | bytes 6291464 | tf_op jit(solution)/shard_map/ppermute | solution.py:13
  69.9 91.0 %collective-permute-start.1 = (bf16[2,2,256,1024]{2,3,1,0:T(8,128)(2,1)S(1)}, bf16[2,2,256,1024]{2,3,1,0:T(8,128)(2,1)S(1)}, u32[]{:S(2)}, u32[]{:S(2)}) collective-permute-start(bf16[2,2,256,1024]{2,3,1,0:T(8,128)(2,1)S(1)} %broadcast_select_fusion.1), channel_id=1, source_target_pairs={{0,248},{4,252},{8,0},{12,4},{16,8},{20,12},{24,16},{28,20},{32,24... | collective-permute-start | bytes 6291464 | tf_op jit(solution)/shard_map/ppermute | solution.py:13
  161.2 91.9 %collective-permute-start.2 = (bf16[2,2,256,1024]{2,3,1,0:T(8,128)(2,1)S(1)}, bf16[2,2,256,1024]{2,3,1,0:T(8,128)(2,1)S(1)}, u32[]{:S(2)}, u32[]{:S(2)}) collective-permute-start(bf16[2,2,256,1024]{2,3,1,0:T(8,128)(2,1)S(1)} %broadcast_select_fusion.2), channel_id=1, source_target_pairs={{0,240},{4,244},{8,248},{12,252},{16,0},{20,4},{24,8},{28,12},{32,... | collective-permute-start | bytes 6291464 | tf_op jit(solution)/shard_map/ppermute | solution.py:13
  254.7 1.6 copy-start.2
  362.0 52.3 %collective-permute-start.3 = (bf16[2,2,256,1024]{2,3,1,0:T(8,128)(2,1)S(1)}, bf16[2,2,256,1024]{2,3,1,0:T(8,128)(2,1)S(1)}, u32[]{:S(2)}, u32[]{:S(2)}) collective-permute-start(bf16[2,2,256,1024]{2,3,1,0:T(8,128)(2,1)S(1)} %bitcast.134), channel_id=1, source_target_pairs={{0,252},{4,0},{8,4},{12,8},{16,12},{20,16},{24,20},{28,24},{32,28}... | collective-permute-start | bytes 6291464 | tf_op jit(solution)/shard_map/ppermute | solution.py:13
  414.3 105.6 %copy-start.5 = (bf16[2,2,256,1024]{2,3,1,0:T(8,128)(2,1)}, bf16[2,2,256,1024]{2,3,1,0:T(8,128)(2,1)S(1)}, u32[]{:S(2)}) copy-start(bf16[2,2,256,1024]{2,3,1,0:T(8,128)(2,1)S(1)} %collective-permute-done.3) | copy-start | bytes 6291460
  414.3 52.4 %collective-permute-start.4 = (bf16[2,2,256,1024]{2,3,1,0:T(8,128)(2,1)S(1)}, bf16[2,2,256,1024]{2,3,1,0:T(8,128)(2,1)S(1)}, u32[]{:S(2)}, u32[]{:S(2)}) collective-permute-start(bf16[2,2,256,1024]{2,3,1,0:T(8,128)(2,1)S(1)} %collective-permute-done.3), channel_id=1, source_target_pairs={{0,252},{4,0},{8,4},{12,8},{16,12},{20,16},{24,20},{28,24},{32,28}... | collective-permute-start | bytes 6291464 | tf_op jit(solution)/shard_map/ppermute | solution.py:13
  466.7 1.4 copy-start.4
  468.1 51.8 %collective-permute-start.5 = (bf16[2,2,256,1024]{2,3,1,0:T(8,128)(2,1)S(1)}, bf16[2,2,256,1024]{2,3,1,0:T(8,128)(2,1)}, u32[]{:S(2)}, u32[]{:S(2)}) collective-permute-start(bf16[2,2,256,1024]{2,3,1,0:T(8,128)(2,1)S(1)} %collective-permute-done.4), channel_id=1, source_target_pairs={{0,252},{4,0},{8,4},{12,8},{16,12},{20,16},{24,20},{28,24},{32,28}... | collective-permute-start | bytes 6291464 | tf_op jit(solution)/shard_map/ppermute | solution.py:13
  519.9 122.5 %collective-permute-start.6 = (bf16[2,2,256,1024]{2,3,1,0:T(8,128)(2,1)}, bf16[2,2,256,1024]{2,3,1,0:T(8,128)(2,1)}, u32[]{:S(2)}, u32[]{:S(2)}) collective-permute-start(bf16[2,2,256,1024]{2,3,1,0:T(8,128)(2,1)} %collective-permute-done.5), channel_id=1, source_target_pairs={{0,252},{4,0},{8,4},{12,8},{16,12},{20,16},{24,20},{28,24},{32,28}... | collective-permute-start | bytes 6291464 | tf_op jit(solution)/shard_map/ppermute | solution.py:13
  531.6 43.6 %copy-start.3 = (bf16[2,2,256,1024,1]{2,1,3,4,0:T(2,128)(2,1)S(1)}, bf16[2,2,256,1024,1]{2,1,3,4,0:T(2,128)(2,1)}, u32[]{:S(2)}) copy-start(bf16[2,2,256,1024,1]{2,1,3,4,0:T(2,128)(2,1)} %copy.126) | copy-start | bytes 6291460
  642.4 134.9 %collective-permute-start.7 = (bf16[2,2,256,1024]{2,3,1,0:T(8,128)(2,1)}, bf16[2,2,256,1024]{2,3,1,0:T(8,128)(2,1)}, u32[]{:S(2)}, u32[]{:S(2)}) collective-permute-start(bf16[2,2,256,1024]{2,3,1,0:T(8,128)(2,1)} %collective-permute-done.6), channel_id=1, source_target_pairs={{0,252},{4,0},{8,4},{12,8},{16,12},{20,16},{24,20},{28,24},{32,28}... | collective-permute-start | bytes 6291464 | tf_op jit(solution)/shard_map/ppermute | solution.py:13
  777.3 134.7 %collective-permute-start.8 = (bf16[2,2,256,1024]{2,3,1,0:T(8,128)(2,1)}, bf16[2,2,256,1024]{2,3,1,0:T(8,128)(2,1)}, u32[]{:S(2)}, u32[]{:S(2)}) collective-permute-start(bf16[2,2,256,1024]{2,3,1,0:T(8,128)(2,1)} %collective-permute-done.7), channel_id=1, source_target_pairs={{0,252},{4,0},{8,4},{12,8},{16,12},{20,16},{24,20},{28,24},{32,28}... | collective-permute-start | bytes 6291464 | tf_op jit(solution)/shard_map/ppermute | solution.py:13
  935.9 54.3 %copy-start.1 = (bf16[2,2,1,256,1024]{4,3,2,1,0:T(8,128)(2,1)S(1)}, bf16[2,2,1,256,1024]{4,3,2,1,0:T(8,128)(2,1)}, u32[]{:S(2)}) copy-start(bf16[2,2,1,256,1024]{4,3,2,1,0:T(8,128)(2,1)} %param.7) | copy-start | bytes 6291460
Sparse Core Ops, SparseCore 0:
  254.9 95.1 all-gather.1
where the time goes:
time: 1010 us; the launch traced here: 997 us
  waiting for transfers between devices  450 us (45%)
  local copies, waits for them, and re-layouts  326 us (32%)
  matrix products  141 us (14%)
  starting transfers between devices  45.4 us (4%)
  between operations  14.7 us (1%)
  other arithmetic  13.8 us (1%)
    ppermute x9, waiting for transfers between devices, passed_along(): return lax.ppermute(value, axis, pairs)  358 us
    dynamic_slice x14, local copies, waits for them, and re-layouts, partial_trace(): square = lax.dynamic_slice_in_dim(block, offset, local_rows, 3)  292 us
    dot_general x6, matrix products, complex_rect(): jnp.einsum('kcrn,ldrn->kcld', source, sink, preferred_element_type=jnp.fl...  134 us
    all_gather x1, waiting for transfers between devices, on_device(): piece = lax.all_gather(moving, 'mode', axis=2, tiled=True)  91.7 us
    ppermute x9, starting transfers between devices, passed_along(): return lax.ppermute(value, axis, pairs)  45.4 us
  transfers between devices with their start and end apart: 10, of which 7 were waited for; matrix products, arithmetic and copies ran while one was open for 39% of the time, Pallas kernels for 0%

commit v1 on v0

v1 whole, which is shorter than its diff:
```python
import functools

import jax
import jax.numpy as jnp
from jax import lax
from jax.experimental import pallas as pl
from jax.experimental.pallas import tpu as pltpu
from jax.sharding import PartitionSpec as P

HALF = 3
DMAX = 7
MESH = pl.DeviceIdType.MESH
DMA = pltpu.SemaphoreType.DMA
T = 64
RING = 8
ROWS = 256
N = 1024
CHUNKS = 4
WIDE = N // CHUNKS
STEPS = 2 * CHUNKS
MIB = 2**20


def remote(src, dst, send, recv, device):
    return pltpu.make_async_remote_copy(
        src_ref=src, dst_ref=dst, send_sem=send, recv_sem=recv, device_id=device, device_id_type=MESH
    )


def greet(devices):
    barrier = pltpu.get_barrier_semaphore()
    for device in devices:
        pl.semaphore_signal(barrier, inc=1, device_id=device, device_id_type=MESH)
    pl.semaphore_wait(barrier, len(devices))


def meet_kernel(
    offset, first_ref, left_ref, right_ref, out_ref, sent, whole, s1, r1, s2, r2, s3, r3, s4, r4
):
    t, m = lax.axis_index("tm"), lax.axis_index("mode")
    across = (t, lax.rem(m + 2, 4))
    core = (t, m + 1 - 2 * lax.rem(m, 2))
    targets, sources = [], []
    for shift in (DMAX, offset):
        later, earlier = lax.rem(t + shift, T), lax.rem(t + T - shift, T)
        flip_in = lax.rem(t // RING + later // RING, 2)
        flip_out = lax.rem(t // RING + earlier // RING, 2)
        sources.append((later, lax.rem(m + 2 * flip_in, 4)))
        targets.append((earlier, lax.rem(m + 2 * flip_out, 4)))
    greet([sources[0], sources[1], across, core])

    first = first_ref[0]

    def field(product):
        return first if product == 0 else 1 - first

    def rows_of(mode):
        return pl.ds(pl.multiple_of(mode * ROWS, ROWS), ROWS)

    def block(step, mode):
        return whole.at[step, :, rows_of(mode), :]

    def shifted(step, product):
        return remote(sent.at[step], block(step, m), s1.at[step], r1.at[step], targets[product])

    def over_chips(step, product):
        part = block(step, sources[product][1])
        return remote(part, part, s2.at[step], r2.at[step], across)

    def over_cores(step, product):
        part = block(step, sources[product][1])
        return remote(part, part, s3.at[step], r3.at[step], core)

    def over_cores_late(step, product):
        part = block(step, lax.rem(sources[product][1] + 2, 4))
        return remote(part, part, s4.at[step], r4.at[step], core)

    for step in range(STEPS):
        product, column = step % 2, step // 2
        sent[step] = right_ref[field(product), :, :, column * WIDE : (column + 1) * WIDE]
        shifted(step, product).start()

    def multiply(column, product):
        step = 2 * column + product
        over_cores(step, product).wait_recv()
        over_cores_late(step, product).wait_recv()
        real_left, imag_left = left_ref[field(product), 0], left_ref[field(product), 1]
        real_right, imag_right = whole[step, 0], whole[step, 1]
        dot = functools.partial(jnp.dot, preferred_element_type=jnp.float32)
        real = dot(real_left, real_right) - dot(imag_left, imag_right)
        imag = dot(real_left, imag_right) + dot(imag_left, real_right)
        pieces = jnp.concatenate(
            [real.reshape(ROWS // 8, 8, WIDE), imag.reshape(ROWS // 8, 8, WIDE)], axis=1
        ).astype(jnp.bfloat16)
        place = pl.ds(pl.multiple_of((column // 2) * 32, 32), 32)
        lanes = pl.ds(pl.multiple_of(lax.rem(column, 2) * WIDE, WIDE), WIDE)
        out_ref[product, place, :, lanes] = pieces

    def turn(i, _):
        @pl.when(i < CHUNKS)
        def _():
            for product in range(2):
                shifted(2 * i + product, product).wait_recv()
                over_chips(2 * i + product, product).start()
                over_cores(2 * i + product, product).start()

        @pl.when((i >= 1) & (i < CHUNKS + 1))
        def _():
            for product in range(2):
                over_chips(2 * (i - 1) + product, product).wait_recv()
                over_cores_late(2 * (i - 1) + product, product).start()

        @pl.when(i >= 2)
        def _():
            for product in range(2):
                multiply(i - 2, product)

        return 0

    lax.fori_loop(0, CHUNKS + 2, turn, 0)

    def finish(i, _):
        for product in range(2):
            for copy in (shifted, over_chips, over_cores, over_cores_late):
                copy(2 * i + product, product).wait_send()
        return 0

    lax.fori_loop(0, CHUNKS, finish, 0)


def meet(offset, collective, first, left, right):
    vmem = pl.BlockSpec(memory_space=pltpu.VMEM)
    return pl.pallas_call(
        functools.partial(meet_kernel, offset),
        out_shape=jax.ShapeDtypeStruct((2, T, 16, 512), jnp.bfloat16),
        in_specs=[pl.BlockSpec(memory_space=pltpu.SMEM), vmem, vmem],
        out_specs=vmem,
        scratch_shapes=[
            pltpu.VMEM((STEPS, 2, ROWS, WIDE), jnp.bfloat16),
            pltpu.VMEM((STEPS, 2, N, WIDE), jnp.bfloat16),
        ]
        + [DMA((STEPS,))] * 8,
        compiler_params=pltpu.CompilerParams(
            collective_id=collective, has_side_effects=True, vmem_limit_bytes=48 * MIB
        ),
    )(first, left, right)


def spread_lanes(value):
    row = lax.broadcasted_iota(jnp.int32, value.shape, 0)
    for bit in range(6):
        use = lax.rem(row // (1 << bit), 2) == 1
        value = jnp.where(use, pltpu.roll(value, 128 - (2 << bit), 1), value)
    return value


def gram_kernel(
    in_ref, out_ref, got, wide, part_a, part_b, part_c, own, sa, ra, sb, rb, sc, rc, sd, rd
):
    t, m = lax.axis_index("tm"), lax.axis_index("mode")
    z, ring = lax.rem(t, RING), t // RING
    barrier = pltpu.get_barrier_semaphore()

    def hello(i, _):
        pl.semaphore_signal(
            barrier, inc=1, device_id=(lax.rem(t + i, T), m), device_id_type=MESH
        )
        return 0

    lax.fori_loop(1, T, hello, 0)
    for i in range(1, 4):
        pl.semaphore_signal(
            barrier, inc=1, device_id=(t, lax.rem(m + i, 4)), device_id_type=MESH
        )
    pl.semaphore_wait(barrier, T - 1 + 3)

    def send(i, _):
        odd = lax.rem(i, 2)
        ahead = odd * ((i + 1) // 2) + (1 - odd) * (T - i // 2)
        to = lax.rem(t + ahead, T)
        remote(in_ref.at[:, to], got.at[:, t], sa, ra, (to, m)).start()
        return 0

    lax.fori_loop(1, T, send, 0)
    got[:, t] = in_ref[:, t]
    remote(in_ref.at[:, pl.ds(0, T - 1)], got.at[:, pl.ds(0, T - 1)], sa, ra, (lax.rem(t + 1, T), m)).wait()

    rows = 2 * T * 16
    for j in range(4):
        piece = got[:, :, :, j * 128 : (j + 1) * 128].astype(jnp.float32)
        wide[pl.ds(j * rows, rows), :] = piece.reshape(rows, 128)

    def strided(start, count, stride):
        pieces = [wide[pl.ds(j * rows + start, count, stride=stride), :] for j in range(4)]
        return jnp.concatenate(pieces, axis=1).astype(jnp.bfloat16)

    lane = lax.broadcasted_iota(jnp.int32, (16, 512), 1) + (t // 32) * 512
    grams = jnp.zeros((256, 256), jnp.float32)
    traces = jnp.zeros((16, 256), jnp.float32)
    for r in range(8):
        right = strided(r, 256, 8)
        left = jnp.concatenate([strided(r, 128, 16), strided(r + 8, 128, 16)], axis=0)
        diagonal = jnp.where(lane == m * ROWS + lax.rem(t, 32) * 8 + r, 1.0, 0.0).astype(jnp.bfloat16)
        over_lanes = (((1,), (1,)), ((), ()))
        grams += lax.dot_general(left, right, over_lanes, preferred_element_type=jnp.float32)
        traces += lax.dot_general(diagonal, right, over_lanes, preferred_element_type=jnp.float32)

    place = lax.broadcasted_iota(jnp.int32, (T, 128), 1) // 16
    packed = jnp.zeros((T, 128), jnp.float32)
    packed_traces = jnp.zeros((T, 128), jnp.float32)
    for c in range(2):
        for p in range(2):
            for l in range(2):
                index = c * 4 + p * 2 + l
                top = c * 128 + p * 64
                value = spread_lanes(grams[top : top + 64, l * 128 : (l + 1) * 128])
                value = pltpu.roll(value, 16 * index, 1) if index else value
                packed = jnp.where(place == index, value, packed)
    for l in range(2):
        value = jnp.broadcast_to(traces[0:1, l * 128 : (l + 1) * 128], (T, 128))
        value = spread_lanes(value)
        value = pltpu.roll(value, 16 * l, 1) if l else value
        packed_traces = jnp.where(place == l, value, packed_traces)
    own[:, :, 0:128] = packed.reshape(8, 8, 128)
    own[:, :, 128:256] = packed_traces.reshape(8, 8, 128)

    copies = []
    for i in range(1, 8):
        to = lax.rem(ring + i, 8)
        copies.append(remote(own.at[to], part_a.at[ring], sb.at[i], rb.at[i], (to * RING + z, m)))
    for copy in copies:
        copy.start()
    part_a[ring] = own[ring]
    for copy in copies:
        copy.wait()
    own[0] = jnp.sum(part_a[...], axis=0)

    copies = []
    for i in range(1, 8):
        to = lax.rem(z + i, 8)
        copies.append(remote(own.at[0], part_b.at[z], sc.at[i], rc.at[i], (ring * RING + to, m)))
    for copy in copies:
        copy.start()
    part_b[z] = own[0]
    for copy in copies:
        copy.wait()
    own[1] = jnp.sum(part_b[...], axis=0)

    copies = []
    for i in range(1, 4):
        to = lax.rem(m + i, 4)
        copies.append(remote(own.at[1], part_c.at[m], sd.at[i], rd.at[i], (t, to)))
    for copy in copies:
        copy.start()
    part_c[m] = own[1]
    for copy in copies:
        copy.wait()
    out_ref[...] = part_c[0] + part_c[1] + part_c[2] + part_c[3]


def gram(products):
    vmem = pl.BlockSpec(memory_space=pltpu.VMEM)
    return pl.pallas_call(
        gram_kernel,
        out_shape=jax.ShapeDtypeStruct((8, 256), jnp.float32),
        in_specs=[vmem],
        out_specs=vmem,
        scratch_shapes=[
            pltpu.VMEM((2, T, 16, 512), jnp.bfloat16),
            pltpu.VMEM((4 * 2 * T * 16, 128), jnp.float32),
            pltpu.VMEM((8, 8, 256), jnp.float32),
            pltpu.VMEM((8, 8, 256), jnp.float32),
            pltpu.VMEM((4, 8, 256), jnp.float32),
            pltpu.VMEM((8, 8, 256), jnp.float32),
            DMA, DMA, DMA((8,)), DMA((8,)), DMA((8,)), DMA((8,)), DMA((4,)), DMA((4,)),
        ],
        compiler_params=pltpu.CompilerParams(
            collective_id=0, has_side_effects=True, vmem_limit_bytes=48 * MIB
        ),
    )(products)


def on_device(fields_left, fields_right, delta, pair):
    left, right = fields_left[:, :, 0], fields_right[:, :, 0]
    largest = jnp.argmax(delta).astype(jnp.int32)
    first = pair[largest].reshape(1)
    other = delta[1 - largest]
    branches = [functools.partial(meet, offset, offset) for offset in range(1, DMAX)]
    products = lax.switch(other - 1, branches, first, left, right)
    sums = gram(products)
    z = lax.rem(lax.axis_index("tm"), RING)
    row = lax.dynamic_slice_in_dim(sums, z, 1, 0)[0]
    order = jnp.where(jnp.arange(2) == largest, 0, 1)
    grams = row[:128].reshape(2, 2, 2, 8, 2)
    grams = grams[:, :, :, 1:7][:, order][:, :, order]
    rect_real = grams[0, ..., 0] + grams[1, ..., 1]
    rect_imag = grams[1, ..., 0] - grams[0, ..., 1]
    traces = row[128:160].reshape(2, 8, 2)[order]
    here = traces[:, 0][:, None, None, :]
    there = traces[:, 1:7][None]
    box_real = here[..., 0] * there[..., 0] + here[..., 1] * there[..., 1]
    box_imag = here[..., 1] * there[..., 0] - here[..., 0] * there[..., 1]
    rectangle = jnp.stack([rect_real, rect_imag]) / N
    box = jnp.stack([box_real, box_imag]) / N
    return rectangle[None], box[None]


def solution(mesh):
    split = P(None, None, "tm", "mode", None)
    out = P("tm", None, None, None, None)
    return jax.shard_map(
        on_device, mesh=mesh, in_specs=(split, split, P(), P()), out_specs=(out, out), check_vma=False
    )
```

time: 1010 us -> 179 us (0.18); the launches traced: 997 us -> 179 us
  waiting for transfers between devices: 450 us -> 0 us
  local copies, waits for them, and re-layouts: 326 us -> 5.07 us
  Pallas kernels: 0 us -> 166 us
  matrix products: 141 us -> 0 us
  starting transfers between devices: 45.4 us -> 0 us
  other arithmetic: 13.8 us -> 2.73 us
    ppermute x9 -> x0, waiting for transfers between devices: 358 us -> none  [passed_along(): return lax.ppermute(value, axis, pairs)]
    dynamic_slice x14 -> x2, local copies, waits for them, and re-layouts: 292 us -> 2.56 us  [the longest x1 1.32 us: on_device(): first = pair[largest].reshape(1)]
    pallas_call x0 -> x2, Pallas kernels: none -> 166 us  [the longest x1 92.5 us: meet(): pl.pallas_call(functools.partial(meet_kernel, offset), out_shape=jax.Shap...]
    dot_general x7 -> x0, matrix products: 141 us -> none  [the longest x6 134 us: complex_rect(): jnp.einsum('kcrn,ldrn->kcld', source, sink, preferred_element_type=jnp.fl...]
    all_gather x1 -> x0, waiting for transfers between devices: 91.7 us -> none  [on_device(): piece = lax.all_gather(moving, 'mode', axis=2, tiled=True)]
    ppermute x9 -> x0, starting transfers between devices: 45.4 us -> none  [passed_along(): return lax.ppermute(value, axis, pairs)]
    gather x10 -> x3, local copies, waits for them, and re-layouts: 24.2 us -> 1.66 us  [the longest x2 1.1 us: on_device(): grams = grams[:, :, :, 1:7][:, order][:, :, order]]
  transfers between devices with their start and end apart: 10 -> 0, of which waited for: 7 -> 0; matrix products, arithmetic and copies ran while one was open for 39% -> 0% of each run, Pallas kernels for 0% -> 0%
where the time goes in v1:
time: 179 us
  Pallas kernels  166 us (93%)
  local copies, waits for them, and re-layouts  5.07 us (3%)
  between operations  4.62 us (3%)
  other arithmetic  2.73 us (2%)
    pallas_call x1, Pallas kernels, meet(): pl.pallas_call(functools.partial(meet_kernel, offset), out_shape=jax.Shap...  92.5 us
    pallas_call x1, Pallas kernels, gram(): pl.pallas_call(gram_kernel, out_shape=jax.ShapeDtypeStruct((8, 256), jnp....  73.7 us

profile of v1, /device:TPU:1, one launch (start us, length us, event | category | flops | bytes accessed | tf_op | source)
XLA Modules:
  0.0 178.9 jit_solution(1764458834074148518)
XLA Ops:
  0.6 1.3 iota_reduce_fusion
  3.2 1.2 dynamic_slice.9
  7.1 1.3 dynamic_slice.10
  8.4 92.7 %conditional.1 = (bf16[2,64,16,512]{3,2,1,0:T(8,128)(2,1)S(1)}) conditional(s32[]{:T(128)} %bitcast, (s32[1]{0:T(128)}, bf16[2,2,256,1024]{3,2,1,0:T(8,128)(2,1)}, bf16[2,2,256,1024]{3,2,1,0:T(8,128)(2,1)}) %tuple.47, (s32[1]{0:T(128)}, bf16[2,2,256,1024]{3,2,1,0:T(8,128)(2,1)}, ...), branch_computations={%region_1.2_spmd, %region_2.3_spmd, %region_3.4_spmd, %region_4.5_... | conditional | bytes 8 | solution.py:289
  8.4 92.5 %branch_2_fun.1 = bf16[2,64,16,512]{3,2,1,0:T(8,128)(2,1)S(1)} custom-call(s32[1]{0:T(128)} %get-tuple-element.49.first_ref, bf16[2,2,256,1024]{3,2,1,0:T(8,128)(2,1)} %get-tuple-element.50.left_ref, bf16[2,2,256,1024]{3,2,1,0:T(8,128)(2,1)} %get-tuple-element.51.right_ref), custom_call_target="tpu_custom_call" | custom-call | tf_op jit(solution)/shard_map/cond/branch_2_fun/pallas_call | solution.py:133
  101.1 73.7 %shard_map.59 = f32[8,256]{1,0:T(8,128)S(1)} custom-call(bf16[2,64,16,512]{3,2,1,0:T(8,128)(2,1)S(1)} %get-tuple-element.75.in_ref), custom_call_target="tpu_custom_call" | custom-call | tf_op jit(solution)/shard_map/pallas_call | solution.py:263
  174.9 0.1 reshape.147
  175.0 0.7 fusion
  175.7 0.5 gather_fusion
  176.3 0.5 gather_fusion.1
  176.8 0.1 slice_add_fusion
  176.9 0.1 copy.10
  177.0 0.1 copy.9
  177.1 0.1 dynamic-slice_reduce_fusion
  177.2 0.1 reshape.148
  177.3 0.6 gather_fusion.2
  177.9 0.1 copy.11
  178.0 0.2 slice_reduce_fusion.1
  178.2 0.1 add_bitcast_fusion
  178.2 0.6 maximum_multiply_fusion
  (6 shorter events, 0.0 us)

commit v2 on v0

v2 whole, which is shorter than its diff:
```python
import functools

import jax
import jax.numpy as jnp
from jax import lax
from jax.experimental import pallas as pl
from jax.experimental.pallas import tpu as pltpu
from jax.sharding import PartitionSpec as P

HALF = 3
DMAX = 7
MESH = pl.DeviceIdType.MESH
DMA = pltpu.SemaphoreType.DMA
T = 64
RING = 8
ROWS = 256
N = 1024
CHUNKS = 4
WIDE = N // CHUNKS
STEPS = 2 * CHUNKS
MIB = 2**20


def remote(src, dst, send, recv, device):
    return pltpu.make_async_remote_copy(
        src_ref=src, dst_ref=dst, send_sem=send, recv_sem=recv, device_id=device, device_id_type=MESH
    )


def rolled_rows(value):
    row = lax.broadcasted_iota(jnp.int32, value.shape, 0)
    for bit in range(6):
        use = lax.rem(row // (1 << bit), 2) == 1
        value = jnp.where(use, pltpu.roll(value, 128 - (2 << bit), 1), value)
    return value


def lanes_of(shape, axis):
    return lax.broadcasted_iota(jnp.int32, shape, axis)


def fused_kernel(
    offset, ahead, delta_ref, pair_ref, left_ref, right_ref, out_ref,
    left_in, right_in, left_op, left_sent, sent, whole, made, got, wide, folded, grams, picks,
    own, part_a, part_b, part_c, last,
    in_sem, sl, rl, s1, r1, s2, r2, s3, r3, s4, r4, sa, ra, sb, rb, sc, rc, sd, rd,
):
    t, m = lax.axis_index("tm"), lax.axis_index("mode")
    z, ring = lax.rem(t, RING), t // RING
    moves = (DMAX, (offset - ahead) % T)
    loads = [
        pltpu.make_async_copy(right_ref, right_in, in_sem.at[0]),
        pltpu.make_async_copy(left_ref, left_in, in_sem.at[1]),
    ]
    for load in loads:
        load.start()

    across = (t, lax.rem(m + 2, 4))
    core = (t, m + 1 - 2 * lax.rem(m, 2))
    targets, sources = [], []
    for shift in moves:
        later, earlier = lax.rem(t + shift, T), lax.rem(t + T - shift, T)
        flip_in = lax.rem(t // RING + later // RING, 2)
        flip_out = lax.rem(t // RING + earlier // RING, 2)
        sources.append((later, lax.rem(m + 2 * flip_in, 4)))
        targets.append((earlier, lax.rem(m + 2 * flip_out, 4)))

    barrier = pltpu.get_barrier_semaphore()

    def hello(i, _):
        pl.semaphore_signal(barrier, inc=1, device_id=(lax.rem(t + i, T), m), device_id_type=MESH)
        return 0

    for source in sources:
        pl.semaphore_signal(barrier, inc=1, device_id=source, device_id_type=MESH)
    for i in range(1, 4):
        pl.semaphore_signal(barrier, inc=1, device_id=(t, lax.rem(m + i, 4)), device_id_type=MESH)
    lax.fori_loop(1, T, hello, 0)

    in_order = delta_ref[0] == DMAX
    first = jnp.where(in_order, pair_ref[0], pair_ref[1])

    loads[0].wait()
    for product in range(2):
        field = first if product == 0 else 1 - first
        for column in range(CHUNKS):
            sent[product * CHUNKS + column] = right_in[field, :, :, column * WIDE : (column + 1) * WIDE]
    pl.semaphore_wait(barrier, T - 1 + 3 + 2)

    source_modes = (sources[0][1], sources[1][1])

    def block(step, mode):
        return whole.at[step, :, pl.ds(pl.multiple_of(mode * ROWS, ROWS), ROWS), :]

    def shifted(step, product):
        return remote(sent.at[step], block(step, m), s1.at[step], r1.at[step], targets[product])

    def source_mode(step):
        product = step // CHUNKS
        return source_modes[0] * (1 - product) + source_modes[1] * product

    def over_chips(step):
        part = block(step, source_mode(step))
        return remote(part, part, s2.at[step], r2.at[step], across)

    def over_cores(step):
        part = block(step, source_mode(step))
        return remote(part, part, s3.at[step], r3.at[step], core)

    def over_cores_late(step):
        part = block(step, lax.rem(source_mode(step) + 2, 4))
        return remote(part, part, s4.at[step], r4.at[step], core)

    for column in range(CHUNKS):
        for product in range(2):
            shifted(product * CHUNKS + column, product).start()

    loads[1].wait()
    left_op[0] = left_in[first]
    if ahead == 0:
        left_op[1] = left_in[1 - first]
    else:
        left_sent[...] = left_in[1 - first]
        left_move = remote(left_sent, left_op.at[1], sl, rl, (lax.rem(t + ahead + T, T), m))
        left_move.start()

    def multiply(step):
        product, column = step // CHUNKS, lax.rem(step, CHUNKS)
        over_cores(step).wait_recv()
        over_cores_late(step).wait_recv()
        real_left, imag_left = left_op[product, 0], left_op[product, 1]
        real_right, imag_right = whole[step, 0], whole[step, 1]
        dot = functools.partial(jnp.dot, preferred_element_type=jnp.float32)
        real = dot(real_left, real_right) - dot(imag_left, imag_right)
        imag = dot(real_left, imag_right) + dot(imag_left, real_right)
        pieces = jnp.concatenate(
            [real.reshape(ROWS // 8, 8, WIDE), imag.reshape(ROWS // 8, 8, WIDE)], axis=1
        ).astype(jnp.bfloat16)
        place = pl.ds(pl.multiple_of(lax.rem(column, 2) * 32, 32), 32)
        made[product, column // 2, place] = pieces

    def spread(product, half):
        slot = lax.rem(t + T - ahead * product, T)

        def send(i, _):
            odd = lax.rem(i, 2)
            far = odd * ((i + 1) // 2) + (1 - odd) * (T - i // 2)
            to = lax.rem(t + far, T)
            remote(
                made.at[product, half, to], got.at[product, half, slot],
                sa.at[product, half], ra.at[product, half], (to, m),
            ).start()
            return 0

        lax.fori_loop(1, T, send, 0)
        got[product, half, slot] = made[product, half, t]

    def step_at(turn):
        return turn - turn // 5

    def busy(turn):
        return (turn >= 0) & (turn != 4) & (turn < 9)

    def turn_of(i, _):
        @pl.when(busy(i - 2))
        def _():
            step = step_at(i - 2)
            if ahead != 0:
                @pl.when(step == CHUNKS)
                def _():
                    left_move.wait_recv()
            multiply(step)

            @pl.when(lax.rem(step, 2) == 1)
            def _():
                spread(step // CHUNKS, lax.rem(step, CHUNKS) // 2)

        @pl.when(busy(i - 1))
        def _():
            step = step_at(i - 1)
            over_chips(step).wait_recv()
            over_cores_late(step).start()

        @pl.when(busy(i))
        def _():
            step = step_at(i)
            shifted(step, 0).wait_recv()
            over_chips(step).start()
            over_cores(step).start()

        return 0

    lax.fori_loop(0, 11, turn_of, 0)

    sum_row, lane = lanes_of((256, 128), 0), lanes_of((256, 128), 1)
    part, k, l, s = lane // 24, lax.rem(lane // 12, 2), lax.rem(lane // 6, 2), lax.rem(lane, 6) + 1
    swap = jnp.where(in_order, 0, 1)
    k, l = k + swap - 2 * swap * k, l + swap - 2 * swap * l
    valid = lane < 48

    def pick(index, *terms):
        value = jnp.zeros((256, 128), jnp.float32)
        for where, sign in terms:
            value = value + jnp.where((sum_row == where) & valid, sign, 0.0)
        picks[index] = value

    pair_at = (2 * k + l) * 16 + 2 * s
    sign = jnp.where(part == 0, 1.0, -1.0)
    pick(0, (pair_at + 64 * part, 1.0), (pair_at + 1 + 64 * (1 - part), sign))
    for d in range(2):
        pick(1 + d, (128 + k * 16 + d, 1.0))
        pick(3 + d, (128 + l * 16 + 2 * s + d, 1.0))

    over_lanes = (((1,), (1,)), ((), ()))

    def dot_t(a, b):
        return lax.dot_general(a, b, over_lanes, preferred_element_type=jnp.float32)

    mask_lane = lanes_of((16, WIDE), 1)
    traces = [jnp.zeros((16, 128), jnp.float32) for _ in range(2)]

    def absorb(product, half):
        remote(
            made.at[product, half, pl.ds(0, T - 1)], got.at[product, half, pl.ds(0, T - 1)],
            sa.at[product, half], ra.at[product, half], across,
        ).wait()
        count = T * 16
        for j in range(2):
            piece = got[product, half, :, :, j * 128 : (j + 1) * 128].astype(jnp.float32)
            wide[pl.ds(j * count, count), :] = piece.reshape(count, 128)
        for r in range(8):
            pieces = [wide[pl.ds(j * count + r, 128, stride=8), :] for j in range(2)]
            value = jnp.concatenate(pieces, axis=1).astype(jnp.bfloat16)
            folded[product, half, r] = value
            at = (2 * half + t // 32) * WIDE
            hit = mask_lane + at == m * ROWS + lax.rem(t, 32) * 8 + r
            diagonal = jnp.where(hit, 1.0, 0.0).astype(jnp.bfloat16)
            traces[product] += dot_t(diagonal, value)

    def gram(a, b, half):
        value = jnp.zeros((128, 128), jnp.float32)
        for r in range(8):
            value += dot_t(folded[a, half, r], folded[b, half, r])
        return value

    place = lanes_of((T, 128), 1) // 16

    def fold(a, b, packed):
        for c in range(2):
            index = c * 4 + a * 2 + b
            value = rolled_rows(grams[pl.ds((2 * a + b) * 128 + c, T, stride=2), :])
            value = pltpu.roll(value, 16 * index, 1) if index else value
            packed = jnp.where(place == index, value, packed)
        return packed

    def fold_traces(a, packed):
        value = rolled_rows(jnp.broadcast_to(traces[a][0:1], (T, 128)))
        value = pltpu.roll(value, 16 * a, 1) if a else value
        return jnp.where(place == a, value, packed)

    packed = jnp.zeros((T, 128), jnp.float32)
    packed_traces = jnp.zeros((T, 128), jnp.float32)
    absorb(0, 0)
    grams[0:128, :] = gram(0, 0, 0)
    absorb(0, 1)
    grams[0:128, :] += gram(0, 0, 1)
    packed = fold(0, 0, packed)
    packed_traces = fold_traces(0, packed_traces)
    rest = ((0, 1), (1, 0), (1, 1))
    absorb(1, 0)
    for a, b in rest:
        grams[(2 * a + b) * 128 : (2 * a + b + 1) * 128, :] = gram(a, b, 0)
    absorb(1, 1)
    for a, b in rest:
        grams[(2 * a + b) * 128 : (2 * a + b + 1) * 128, :] += gram(a, b, 1)
    for a, b in rest:
        packed = fold(a, b, packed)
    packed_traces = fold_traces(1, packed_traces)
    own[:, :, 0:128] = packed.reshape(8, 8, 128)
    own[:, :, 128:256] = packed_traces.reshape(8, 8, 128)

    copies = []
    for i in range(1, 8):
        to = lax.rem(ring + i, 8)
        copies.append(remote(own.at[to], part_a.at[ring], sb.at[i], rb.at[i], (to * RING + z, m)))
    for copy in copies:
        copy.start()
    part_a[ring] = own[ring]
    for copy in copies:
        copy.wait()
    part_b[z] = jnp.sum(part_a[...], axis=0)

    copies = []
    for i in range(1, 8):
        to = lax.rem(z + i, 8)
        copies.append(remote(part_b.at[z], part_b.at[z], sc.at[i], rc.at[i], (ring * RING + to, m)))
    for copy in copies:
        copy.start()
    for copy in copies:
        copy.wait()
    part_c[m] = jnp.sum(part_b[...], axis=0)

    copies = []
    for i in range(1, 4):
        to = lax.rem(m + i, 4)
        copies.append(remote(part_c.at[m], part_c.at[m], sd.at[i], rd.at[i], (t, to)))
    for copy in copies:
        copy.start()
    for copy in copies:
        copy.wait()
    last[...] = part_c[0] + part_c[1] + part_c[2] + part_c[3]

    row = jnp.broadcast_to(last[pl.ds(z, 1), :], (8, 256))

    def chosen(index):
        return jnp.dot(
            row, picks[index], preferred_element_type=jnp.float32, precision=lax.Precision.HIGHEST
        )

    here, there = (chosen(1), chosen(2)), (chosen(3), chosen(4))
    box_real = here[0] * there[0] + here[1] * there[1]
    box_imag = here[1] * there[0] - here[0] * there[1]
    box = jnp.where(lanes_of((8, 128), 1) < 24, box_real, box_imag)
    out_ref[...] = jnp.where(lanes_of((8, 128), 0) == 0, chosen(0), box) * (1.0 / N)

    def finish(step, _):
        shifted(step, 0).wait_send()
        for copy in (over_chips, over_cores, over_cores_late):
            copy(step).wait_send()
        return 0

    lax.fori_loop(0, STEPS, finish, 0)
    if ahead != 0:
        left_move.wait_send()


def fused(offset, ahead, delta, pair, left, right):
    vmem = pl.BlockSpec(memory_space=pltpu.VMEM)
    smem = pl.BlockSpec(memory_space=pltpu.SMEM)
    whole = pl.BlockSpec(memory_space=pl.ANY)
    half_float, single = jnp.bfloat16, jnp.float32
    return pl.pallas_call(
        functools.partial(fused_kernel, offset, ahead),
        out_shape=jax.ShapeDtypeStruct((8, 128), single),
        in_specs=[smem, smem, whole, whole],
        out_specs=vmem,
        scratch_shapes=[
            pltpu.VMEM((2, 2, ROWS, N), half_float),
            pltpu.VMEM((2, 2, ROWS, N), half_float),
            pltpu.VMEM((2, 2, ROWS, N), half_float),
            pltpu.VMEM((2, ROWS, N), half_float),
            pltpu.VMEM((STEPS, 2, ROWS, WIDE), half_float),
            pltpu.VMEM((STEPS, 2, N, WIDE), half_float),
            pltpu.VMEM((2, 2, T, 16, WIDE), half_float),
            pltpu.VMEM((2, 2, T, 16, WIDE), half_float),
            pltpu.VMEM((2 * T * 16, 128), single),
            pltpu.VMEM((2, 2, 8, 128, WIDE), half_float),
            pltpu.VMEM((4 * 128, 128), single),
            pltpu.VMEM((5, 256, 128), single),
            pltpu.VMEM((8, 8, 256), single),
            pltpu.VMEM((8, 8, 256), single),
            pltpu.VMEM((8, 8, 256), single),
            pltpu.VMEM((4, 8, 256), single),
            pltpu.VMEM((8, 256), single),
            DMA((2,)), DMA, DMA,
        ]
        + [DMA((STEPS,))] * 8
        + [DMA((2, 2))] * 2
        + [DMA((8,))] * 4
        + [DMA((4,))] * 2,
        compiler_params=pltpu.CompilerParams(
            collective_id=offset, has_side_effects=True, vmem_limit_bytes=48 * MIB
        ),
    )(delta, pair, left, right)


AHEAD = {1: 0, 2: 0, 3: 1, 4: 0, 5: -2, 6: -1}


def on_device(fields_left, fields_right, delta, pair):
    left, right = fields_left[:, :, 0], fields_right[:, :, 0]
    branches = [functools.partial(fused, offset, AHEAD[offset]) for offset in range(1, DMAX)]
    sums = lax.switch(delta[0] + delta[1] - DMAX - 1, branches, delta, pair, left, right)
    shape = (1, 2, 2, 2, 2 * HALF)
    return sums[0, :48].reshape(shape), sums[1, :48].reshape(shape)


def solution(mesh):
    split = P(None, None, "tm", "mode", None)
    out = P("tm", None, None, None, None)
    return jax.shard_map(
        on_device, mesh=mesh, in_specs=(split, split, P(), P()), out_specs=(out, out), check_vma=False
    )
```

time: 1010 us -> 166 us (0.16); the launches traced: 997 us -> 165 us
  waiting for transfers between devices: 450 us -> 0 us
  local copies, waits for them, and re-layouts: 326 us -> 2.7 us
  Pallas kernels: 0 us -> 160 us
  matrix products: 141 us -> 0 us
  starting transfers between devices: 45.4 us -> 0 us
  other arithmetic: 13.8 us -> 0 us
  between operations: 14.7 us -> 1.94 us
    ppermute x9 -> x0, waiting for transfers between devices: 358 us -> none  [passed_along(): return lax.ppermute(value, axis, pairs)]
    dynamic_slice x14 -> x0, local copies, waits for them, and re-layouts: 292 us -> none  [partial_trace(): square = lax.dynamic_slice_in_dim(block, offset, local_rows, 3)]
    pallas_call x0 -> x1, Pallas kernels: none -> 160 us  [fused(): pl.pallas_call(functools.partial(fused_kernel, offset, ahead), out_shape=...]
    dot_general x7 -> x0, matrix products: 141 us -> none  [the longest x6 134 us: complex_rect(): jnp.einsum('kcrn,ldrn->kcld', source, sink, preferred_element_type=jnp.fl...]
    all_gather x1 -> x0, waiting for transfers between devices: 91.7 us -> none  [on_device(): piece = lax.all_gather(moving, 'mode', axis=2, tiled=True)]
    ppermute x9 -> x0, starting transfers between devices: 45.4 us -> none  [passed_along(): return lax.ppermute(value, axis, pairs)]
    gather x10 -> x0, local copies, waits for them, and re-layouts: 24.2 us -> none  [the longest x7 17.3 us: partial_trace(): jnp.diagonal(square, axis1=2, axis2=3).astype(jnp.float32)]
  transfers between devices with their start and end apart: 10 -> 0, of which waited for: 7 -> 0; matrix products, arithmetic and copies ran while one was open for 39% -> 0% of each run, Pallas kernels for 0% -> 0%
where the time goes in v2:
time: 166 us; the launch traced here: 165 us
  Pallas kernels  160 us (96%)
  local copies, waits for them, and re-layouts  2.7 us (2%)
  between operations  1.94 us (1%)
    pallas_call x1, Pallas kernels, fused(): pl.pallas_call(functools.partial(fused_kernel, offset, ahead), out_shape=...  160 us

profile of v2, /device:TPU:1, one launch (start us, length us, event | category | flops | bytes accessed | tf_op | source)
XLA Modules:
  0.0 165.5 jit_solution(9123850806254726370)
XLA Ops:
  0.6 1.3 fusion
  3.2 160.8 %conditional.1 = (f32[8,128]{1,0:T(8,128)S(1)}) conditional(s32[]{:T(128)} %bitcast, (s32[2]{0:T(128)}, s32[2]{0:T(128)}, bf16[2,2,256,1024]{3,2,1,0:T(8,128)(2,1)}, bf16[2,2,256,1024]{3,2,1,0:T(8,128)(2,1)}) %tuple.42, (s32[2]{0:T(128)}, s32[2]{0:T(128)}, bf16[2,2,256,1024]{3,2,1,0:T(8,128)(2,1)}, ...), branch_computations={%region_0.0_spmd, %region_1.0_spmd, %region_2.0_spmd, %region_3.0_... | conditional | bytes 8 | solution.py:383
  3.5 160.3 %branch_3_fun.1 = f32[8,128]{1,0:T(8,128)S(1)} custom-call(s32[2]{0:T(128)} %get-tuple-element.67.delta_ref, s32[2]{0:T(128)} %get-tuple-element.68.pair_ref, bf16[2,2,256,1024]{3,2,1,0:T(8,128)(2,1)} %get-tuple-element.69.left_ref, bf16[2,2,256,1024]{3,2,1,0:T(8,128)(2,1)} %get-tuple-element.70.right_ref), custom_call_target="tpu_custom_call" | custom-call | tf_op jit(solution)/shard_map/cond/branch_3_fun/pallas_call | solution.py:342
  164.1 0.7 reshape_squeeze.7
  164.8 0.7 reshape_squeeze.6
  (1 shorter events, 0.0 us)

commit v3 on v2

--- a/solution.py
+++ b/solution.py
@@ -43,7 +43,7 @@
     offset, ahead, delta_ref, pair_ref, left_ref, right_ref, out_ref,
     left_in, right_in, left_op, left_sent, sent, whole, made, got, wide, folded, grams, picks,
     own, part_a, part_b, part_c, last,
-    in_sem, sl, rl, s1, r1, s2, r2, s3, r3, s4, r4, sa, ra, sb, rb, sc, rc, sd, rd,
+    in_sem, sl, rl, s1, r1, s2, r2, s3, r3, s4, r4, sa, ra, sb, rb, sc, rc,
 ):
     t, m = lax.axis_index("tm"), lax.axis_index("mode")
     z, ring = lax.rem(t, RING), t // RING
@@ -76,6 +76,11 @@
     for i in range(1, 4):
         pl.semaphore_signal(barrier, inc=1, device_id=(t, lax.rem(m + i, 4)), device_id_type=MESH)
     lax.fori_loop(1, T, hello, 0)
+    for i in range(1, 8):
+        other_ring = lax.rem(ring + i, 8) * RING + z
+        other_place = ring * RING + lax.rem(z + i, 8)
+        for device in ((other_ring, core[1]), (other_place, across[1])):
+            pl.semaphore_signal(barrier, inc=1, device_id=device, device_id_type=MESH)
 
     in_order = delta_ref[0] == DMAX
     first = jnp.where(in_order, pair_ref[0], pair_ref[1])
@@ -85,7 +90,7 @@
         field = first if product == 0 else 1 - first
         for column in range(CHUNKS):
             sent[product * CHUNKS + column] = right_in[field, :, :, column * WIDE : (column + 1) * WIDE]
-    pl.semaphore_wait(barrier, T - 1 + 3 + 2)
+    pl.semaphore_wait(barrier, T - 1 + 3 + 2 + 14)
 
     source_modes = (sources[0][1], sources[1][1])
 
@@ -111,7 +116,7 @@
         part = block(step, lax.rem(source_mode(step) + 2, 4))
         return remote(part, part, s4.at[step], r4.at[step], core)
 
-    for column in range(CHUNKS):
+    for column in range(2):
         for product in range(2):
             shifted(product * CHUNKS + column, product).start()
 
@@ -122,7 +127,8 @@
     else:
         left_sent[...] = left_in[1 - first]
         left_move = remote(left_sent, left_op.at[1], sl, rl, (lax.rem(t + ahead + T, T), m))
-        left_move.start()
+        if ahead < 0:
+            left_move.start()
 
     def multiply(step):
         product, column = step // CHUNKS, lax.rem(step, CHUNKS)
@@ -155,16 +161,34 @@
         lax.fori_loop(1, T, send, 0)
         got[product, half, slot] = made[product, half, t]
 
-    def step_at(turn):
-        return turn - turn // 5
-
-    def busy(turn):
-        return (turn >= 0) & (turn != 4) & (turn < 9)
-
     def turn_of(i, _):
-        @pl.when(busy(i - 2))
+        @pl.when(i < STEPS)
         def _():
-            step = step_at(i - 2)
+            shifted(i, 0).wait_recv()
+            over_chips(i).start()
+            over_cores(i).start()
+
+        @pl.when(i < 2)
+        def _():
+            shifted(i + 2, 0).start()
+
+        @pl.when((i >= 2) & (i < 4))
+        def _():
+            shifted(i + 4, 1).start()
+
+        if ahead > 0:
+            @pl.when(i == 2)
+            def _():
+                left_move.start()
+
+        @pl.when((i >= 1) & (i < STEPS + 1))
+        def _():
+            over_chips(i - 1).wait_recv()
+            over_cores_late(i - 1).start()
+
+        @pl.when((i >= 1) & (i != CHUNKS + 1))
+        def _():
+            step = i - 1 - i // (CHUNKS + 2)
             if ahead != 0:
                 @pl.when(step == CHUNKS)
                 def _():
@@ -175,22 +199,9 @@
             def _():
                 spread(step // CHUNKS, lax.rem(step, CHUNKS) // 2)
 
-        @pl.when(busy(i - 1))
-        def _():
-            step = step_at(i - 1)
-            over_chips(step).wait_recv()
-            over_cores_late(step).start()
-
-        @pl.when(busy(i))
-        def _():
-            step = step_at(i)
-            shifted(step, 0).wait_recv()
-            over_chips(step).start()
-            over_cores(step).start()
-
         return 0
 
-    lax.fori_loop(0, 11, turn_of, 0)
+    lax.fori_loop(0, STEPS + 2, turn_of, 0)
 
     sum_row, lane = lanes_of((256, 128), 0), lanes_of((256, 128), 1)
     part, k, l, s = lane // 24, lax.rem(lane // 12, 2), lax.rem(lane // 6, 2), lax.rem(lane, 6) + 1
@@ -279,36 +290,33 @@
     own[:, :, 0:128] = packed.reshape(8, 8, 128)
     own[:, :, 128:256] = packed_traces.reshape(8, 8, 128)
 
-    copies = []
-    for i in range(1, 8):
-        to = lax.rem(ring + i, 8)
-        copies.append(remote(own.at[to], part_a.at[ring], sb.at[i], rb.at[i], (to * RING + z, m)))
-    for copy in copies:
-        copy.start()
-    part_a[ring] = own[ring]
-    for copy in copies:
-        copy.wait()
-    part_b[z] = jnp.sum(part_a[...], axis=0)
-
-    copies = []
-    for i in range(1, 8):
-        to = lax.rem(z + i, 8)
-        copies.append(remote(part_b.at[z], part_b.at[z], sc.at[i], rc.at[i], (ring * RING + to, m)))
-    for copy in copies:
-        copy.start()
-    for copy in copies:
-        copy.wait()
-    part_c[m] = jnp.sum(part_b[...], axis=0)
-
-    copies = []
-    for i in range(1, 4):
-        to = lax.rem(m + i, 4)
-        copies.append(remote(part_c.at[m], part_c.at[m], sd.at[i], rd.at[i], (t, to)))
-    for copy in copies:
-        copy.start()
-    for copy in copies:
-        copy.wait()
-    last[...] = part_c[0] + part_c[1] + part_c[2] + part_c[3]
+    def everyone(buffer, mine, source_of, send, recv, to):
+        copies = []
+        for i in range(1, 16):
+            target, device = to(i)
+            copies.append(remote(source_of(target), buffer.at[mine], send.at[i], recv.at[i], device))
+            copies[-1].start()
+        buffer[mine] = source_of(mine)[...]
+        for copy in copies:
+            copy.wait_recv()
+        total = buffer[0]
+        for i in range(1, 16):
+            total = total + buffer[i]
+        return total, copies
+
+    def over_rings(i):
+        to = lax.rem(mine_a + i, 16)
+        return to, ((to // 2) * RING + z, m // 2 * 2 + lax.rem(to, 2))
+
+    def over_places(i):
+        to = lax.rem(mine_b + i, 16)
+        return to, (ring * RING + to // 2, lax.rem(to, 2) * 2 + lax.rem(m, 2))
+
+    mine_a, mine_b = ring * 2 + lax.rem(m, 2), z * 2 + m // 2
+    total, sent_a = everyone(part_a, mine_a, lambda target: own.at[target // 2], sb, rb, over_rings)
+    part_c[...] = total
+    total, sent_b = everyone(part_b, mine_b, lambda target: part_c, sc, rc, over_places)
+    last[...] = total
 
     row = jnp.broadcast_to(last[pl.ds(z, 1), :], (8, 256))
 
@@ -330,6 +338,8 @@
         return 0
 
     lax.fori_loop(0, STEPS, finish, 0)
+    for copy in sent_a + sent_b:
+        copy.wait_send()
     if ahead != 0:
         left_move.wait_send()
 
@@ -358,16 +368,15 @@
             pltpu.VMEM((4 * 128, 128), single),
             pltpu.VMEM((5, 256, 128), single),
             pltpu.VMEM((8, 8, 256), single),
-            pltpu.VMEM((8, 8, 256), single),
-            pltpu.VMEM((8, 8, 256), single),
-            pltpu.VMEM((4, 8, 256), single),
+            pltpu.VMEM((16, 8, 256), single),
+            pltpu.VMEM((16, 8, 256), single),
+            pltpu.VMEM((8, 256), single),
             pltpu.VMEM((8, 256), single),
             DMA((2,)), DMA, DMA,
         ]
         + [DMA((STEPS,))] * 8
         + [DMA((2, 2))] * 2
-        + [DMA((8,))] * 4
-        + [DMA((4,))] * 2,
+        + [DMA((16,))] * 4,
         compiler_params=pltpu.CompilerParams(
             collective_id=offset, has_side_effects=True, vmem_limit_bytes=48 * MIB
         ),

time: 166 us -> 137 us (0.83)
  Pallas kernels: 160 us -> 131 us
    pallas_call x1, Pallas kernels: 160 us -> 131 us  [fused(): pl.pallas_call(functools.partial(fused_kernel, offset, ahead), out_shape=...]
where the time goes in v3:
time: 137 us; the launch traced here: 136 us
  Pallas kernels  131 us (96%)
  local copies, waits for them, and re-layouts  2.7 us (2%)
  between operations  1.94 us (1%)
    pallas_call x1, Pallas kernels, fused(): pl.pallas_call(functools.partial(fused_kernel, offset, ahead), out_shape=...  131 us

profile of v3, /device:TPU:1, one launch (start us, length us, event | category | flops | bytes accessed | tf_op | source)
XLA Modules:
  0.0 136.4 jit_solution(5552400464615383078)
XLA Ops:
  0.6 1.3 fusion
  3.2 131.8 %conditional.1 = (f32[8,128]{1,0:T(8,128)S(1)}) conditional(s32[]{:T(128)} %bitcast, (s32[2]{0:T(128)}, s32[2]{0:T(128)}, bf16[2,2,256,1024]{3,2,1,0:T(8,128)(2,1)}, bf16[2,2,256,1024]{3,2,1,0:T(8,128)(2,1)}) %tuple.42, (s32[2]{0:T(128)}, s32[2]{0:T(128)}, bf16[2,2,256,1024]{3,2,1,0:T(8,128)(2,1)}, ...), branch_computations={%region_0.0_spmd, %region_1.0_spmd, %region_2.0_spmd, %region_3.0_... | conditional | bytes 8 | solution.py:392
  3.3 131.0 %branch_1_fun.1 = f32[8,128]{1,0:T(8,128)S(1)} custom-call(s32[2]{0:T(128)} %get-tuple-element.54.delta_ref, s32[2]{0:T(128)} %get-tuple-element.60.pair_ref, bf16[2,2,256,1024]{3,2,1,0:T(8,128)(2,1)} %get-tuple-element.61.left_ref, bf16[2,2,256,1024]{3,2,1,0:T(8,128)(2,1)} %get-tuple-element.62.right_ref), custom_call_target="tpu_custom_call" | custom-call | tf_op jit(solution)/shard_map/cond/branch_1_fun/pallas_call | solution.py:352
  135.0 0.7 reshape_squeeze.7
  135.7 0.7 reshape_squeeze.6
  (1 shorter events, 0.0 us)

commit v4 on v3

--- a/solution.py
+++ b/solution.py
@@ -67,15 +67,16 @@
 
     barrier = pltpu.get_barrier_semaphore()
 
-    def hello(i, _):
-        pl.semaphore_signal(barrier, inc=1, device_id=(lax.rem(t + i, T), m), device_id_type=MESH)
+    def hello(to, _):
+        pl.semaphore_signal(barrier, inc=1, device_id=(to, m), device_id_type=MESH)
         return 0
 
     for source in sources:
         pl.semaphore_signal(barrier, inc=1, device_id=source, device_id_type=MESH)
     for i in range(1, 4):
         pl.semaphore_signal(barrier, inc=1, device_id=(t, lax.rem(m + i, 4)), device_id_type=MESH)
-    lax.fori_loop(1, T, hello, 0)
+    lax.fori_loop(t + 1, T, hello, 0)
+    lax.fori_loop(0, t, hello, 0)
     for i in range(1, 8):
         other_ring = lax.rem(ring + i, 8) * RING + z
         other_place = ring * RING + lax.rem(z + i, 8)
@@ -116,9 +117,11 @@
         part = block(step, lax.rem(source_mode(step) + 2, 4))
         return remote(part, part, s4.at[step], r4.at[step], core)
 
+    wait_for_first = offset in FIRST_ALONE
     for column in range(2):
-        for product in range(2):
-            shifted(product * CHUNKS + column, product).start()
+        shifted(column, 0).start()
+        if not wait_for_first:
+            shifted(CHUNKS + column, 1).start()
 
     loads[1].wait()
     left_op[0] = left_in[first]
@@ -148,17 +151,15 @@
     def spread(product, half):
         slot = lax.rem(t + T - ahead * product, T)
 
-        def send(i, _):
-            odd = lax.rem(i, 2)
-            far = odd * ((i + 1) // 2) + (1 - odd) * (T - i // 2)
-            to = lax.rem(t + far, T)
+        def send(to, _):
             remote(
                 made.at[product, half, to], got.at[product, half, slot],
                 sa.at[product, half], ra.at[product, half], (to, m),
             ).start()
             return 0
 
-        lax.fori_loop(1, T, send, 0)
+        lax.fori_loop(t + 1, T, send, 0)
+        lax.fori_loop(0, t, send, 0)
         got[product, half, slot] = made[product, half, t]
 
     def turn_of(i, _):
@@ -171,6 +172,8 @@
         @pl.when(i < 2)
         def _():
             shifted(i + 2, 0).start()
+            if wait_for_first:
+                shifted(i + CHUNKS, 1).start()
 
         @pl.when((i >= 2) & (i < 4))
         def _():
@@ -384,6 +387,7 @@
 
 
 AHEAD = {1: 0, 2: 0, 3: 1, 4: 0, 5: -2, 6: -1}
+FIRST_ALONE = (1, 2, 3, 5, 6)
 
 
 def on_device(fields_left, fields_right, delta, pair):

time: 137 us -> 154 us (1.12)
  Pallas kernels: 131 us -> 149 us
    pallas_call x1, Pallas kernels: 131 us -> 149 us  [fused(): pl.pallas_call(functools.partial(fused_kernel, offset, ahead), out_shape=...]
where the time goes in v4:
time: 154 us
  Pallas kernels  149 us (97%)
  local copies, waits for them, and re-layouts  2.7 us (2%)
  between operations  1.94 us (1%)
    pallas_call x1, Pallas kernels, fused(): pl.pallas_call(functools.partial(fused_kernel, offset, ahead), out_shape=...  149 us

profile of v4, /device:TPU:1, one launch (start us, length us, event | category | flops | bytes accessed | tf_op | source)
XLA Modules:
  0.0 153.9 jit_solution(16827109359477522997)
XLA Ops:
  0.6 1.3 fusion
  3.2 149.3 %conditional.1 = (f32[8,128]{1,0:T(8,128)S(1)}) conditional(s32[]{:T(128)} %bitcast, (s32[2]{0:T(128)}, s32[2]{0:T(128)}, bf16[2,2,256,1024]{3,2,1,0:T(8,128)(2,1)}, bf16[2,2,256,1024]{3,2,1,0:T(8,128)(2,1)}) %tuple.42, (s32[2]{0:T(128)}, s32[2]{0:T(128)}, bf16[2,2,256,1024]{3,2,1,0:T(8,128)(2,1)}, ...), branch_computations={%region_0.0_spmd, %region_1.0_spmd, %region_2.0_spmd, %region_3.0_... | conditional | bytes 8 | solution.py:396
  3.5 148.7 %branch_5_fun.1 = f32[8,128]{1,0:T(8,128)S(1)} custom-call(s32[2]{0:T(128)} %get-tuple-element.75.delta_ref, s32[2]{0:T(128)} %get-tuple-element.76.pair_ref, bf16[2,2,256,1024]{3,2,1,0:T(8,128)(2,1)} %get-tuple-element.77.left_ref, bf16[2,2,256,1024]{3,2,1,0:T(8,128)(2,1)} %get-tuple-element.78.right_ref), custom_call_target="tpu_custom_call" | custom-call | tf_op jit(solution)/shard_map/cond/branch_5_fun/pallas_call | solution.py:355
  152.5 0.7 reshape_squeeze.7
  153.2 0.7 reshape_squeeze.6
  (1 shorter events, 0.0 us)
